TPU v7x, 32 devices: a whole 2x2x4 slice. The times are simulated.
32 devices in a mesh: context: 4 (over z), head: 4 (over y, x), dp: 2 (over core).
Axes of the slice: x: 2, y: 2, z: 4, core: 2. Of those that a mesh axis runs over, the one named last changes fastest.
Arguments:
- query_tok: bfloat16 [2, 2, 512, 5120], P('dp', None, ('context', 'head')), may hold values from -6 to 6
- key_tok: bfloat16 [2, 2, 512, 5120], P('dp', None, ('context', 'head')), may hold values from -6 to 6
- value_tok: bfloat16 [2, 2, 512, 5120], P('dp', None, ('context', 'head')), may hold values from -6 to 6
- token_rates: bfloat16 [2, 2, 512, 40], P('dp', None, ('context', 'head')), may hold values from 0.02 to 3, as said below
- fast_init: bfloat16 [3, 40, 128, 256], P(None, 'head', 'dp'), may hold values from -0.5 to 0.5
- out_gain: bfloat16 [5120], P('head'), may hold values from 0.5 to 1.5
Outputs:
- head_out: bfloat16 [2, 2, 512, 5120], P('dp', None, 'context', 'head')
- fast_final: float32 [2, 3, 40, 128, 256], P('dp', None, 'head')
Inputs may be any that keep to these rules, and one draw needn't show every extreme that they name: `token_rates`: positive learning rates of each token and head.
All inputs are finite; a program needn't handle non-finite values.
Results may differ from a plain program's by a relative error of at most 0.0064.
Values may be sent and summed in bfloat16 or wider, within the bound.
A program may use at most 128 MiB of HBM per device.

v0:
```python
import jax
import jax.numpy as jnp
from jax import lax
from jax.sharding import PartitionSpec as P

BLOCKS = 2
NS_STEPS = 5


schulz_coeffs = (3.4445, -4.775, 2.0315)


def orthogonalize(grads):
    frob = jnp.sqrt(jnp.sum(grads * grads, axis=(1, 2), keepdims=True)) + 1e-07
    ortho = grads / frob
    for sweep in range(NS_STEPS):
        gram = jnp.einsum("nij,nkj->nik", ortho, ortho, precision=lax.Precision.HIGHEST)
        poly = schulz_coeffs[1] * gram + schulz_coeffs[2] * jnp.einsum(
            "nij,njk->nik", gram, gram, precision=lax.Precision.HIGHEST
        )
        ortho = schulz_coeffs[0] * ortho + jnp.einsum(
            "nij,njk->nik", poly, ortho, precision=lax.Precision.HIGHEST
        )
    return ortho


def block_work(queries, keys_blk, vals, rates_blk, fast_state, gain_f):
    weights = fast_state.astype(jnp.bfloat16)
    pre_gate = jnp.einsum("thd,hdf->htf", queries, weights[0], preferred_element_type=jnp.float32)
    pre_up = jnp.einsum("thd,hdf->htf", queries, weights[1], preferred_element_type=jnp.float32)
    hidden_q = (jax.nn.silu(pre_gate) * pre_up).astype(jnp.bfloat16)
    mapped = jnp.einsum("htf,hdf->thd", hidden_q, weights[2], preferred_element_type=jnp.float32)
    mean_sq = jnp.mean(mapped * mapped, axis=-1, keepdims=True)
    normed = (mapped * lax.rsqrt(mean_sq + 1e-06) * gain_f).astype(jnp.bfloat16)
    key_gate = jnp.einsum("thd,hdf->htf", keys_blk, weights[0], preferred_element_type=jnp.float32)
    key_up = jnp.einsum("thd,hdf->htf", keys_blk, weights[1], preferred_element_type=jnp.float32)
    sigma = jax.nn.sigmoid(key_gate)
    act_gate = key_gate * sigma
    slope = sigma * (1.0 + key_gate * (1.0 - sigma))
    hidden_k = (act_gate * key_up).astype(jnp.bfloat16)
    rate_f = rates_blk.astype(jnp.float32)
    rate_col = rate_f.T[:, :, None]
    back = jnp.einsum("thd,hdf->htf", vals, weights[2], preferred_element_type=jnp.float32)
    grad_up_in = (rate_col * back * act_gate).astype(jnp.bfloat16)
    grad_gate_in = (rate_col * back * key_up * slope).astype(jnp.bfloat16)
    rated_value = (rate_f[:, :, None] * vals.astype(jnp.float32)).astype(jnp.bfloat16)
    grads = jnp.stack(
        [
            jnp.einsum("thd,htf->hdf", keys_blk, grad_gate_in, preferred_element_type=jnp.float32),
            jnp.einsum("thd,htf->hdf", keys_blk, grad_up_in, preferred_element_type=jnp.float32),
            jnp.einsum("thd,htf->hdf", rated_value, hidden_k, preferred_element_type=jnp.float32),
        ]
    )
    rate_part = jnp.sum(rate_f, axis=0)
    token_count = queries.shape[0]
    return (normed.reshape(token_count, -1), grads, rate_part)


def body(query_tok, key_tok, value_tok, token_rates, fast_init, out_gain):
    gathered = lax.all_gather(fast_init, "dp", axis=2, tiled=True)
    fast_state = gathered.astype(jnp.float32)
    init_norm = jnp.sqrt(jnp.sum(fast_state * fast_state, axis=2, keepdims=True))
    head_count = gathered.shape[1]
    gain_f = out_gain.astype(jnp.float32).reshape(head_count, -1)
    context_size = lax.axis_size("context")
    arrived = (
        lax.all_to_all(query_tok, "head", split_axis=3, concat_axis=2, tiled=True),
        lax.all_to_all(key_tok, "head", split_axis=3, concat_axis=2, tiled=True),
        lax.all_to_all(value_tok, "head", split_axis=3, concat_axis=2, tiled=True),
        lax.all_to_all(token_rates, "head", split_axis=3, concat_axis=2, tiled=True),
    )
    results = []
    for block_idx in range(BLOCKS):
        pieces = tuple((item[0, block_idx] for item in arrived))
        token_count = pieces[0].shape[0]
        queries = pieces[0].reshape(token_count, head_count, -1)
        keys_blk = pieces[1].reshape(token_count, head_count, -1)
        vals = pieces[2].reshape(token_count, head_count, -1)
        block_out, grads, rate_part = block_work(
            queries, keys_blk, vals, pieces[3], fast_state, gain_f
        )
        results.append(block_out)
        mat_count = 3 * head_count
        flat = grads.reshape(mat_count, grads.shape[2], grads.shape[3])
        rate_total = lax.psum(rate_part, "context")
        per_device = -(-mat_count // context_size)
        pad_count = per_device * context_size - mat_count
        flat = jnp.concatenate(
            [flat, jnp.zeros((pad_count, flat.shape[1], flat.shape[2]), jnp.float32)], axis=0
        )
        own_share = lax.psum_scatter(flat, "context", scatter_dimension=0, tiled=True)
        step_own = orthogonalize(own_share)
        step_all = lax.all_gather(step_own, "context", axis=0, tiled=True)
        step_dir = step_all[:mat_count].reshape(grads.shape)
        step_size = rate_total / (token_count * context_size)
        fast_state = fast_state + step_size[None, :, None, None] * step_dir
        col_norm = jnp.sqrt(jnp.sum(fast_state * fast_state, axis=2, keepdims=True) + 1e-06)
        fast_state = fast_state * (init_norm / col_norm)
    head_out = jnp.stack(results)[None]
    return (head_out, fast_state[None])


def solution(mesh):
    return jax.shard_map(
        body,
        mesh=mesh,
        in_specs=(
            P("dp", None, ("context", "head"), None),
            P("dp", None, ("context", "head"), None),
            P("dp", None, ("context", "head"), None),
            P("dp", None, ("context", "head"), None),
            P(None, "head", "dp", None),
            P("head"),
        ),
        out_specs=(P("dp", None, "context", "head"), P("dp", None, "head", None, None)),
        check_vma=False,
    )
```

profile of v0, /device:TPU:0, one launch (start us, length us, event | category | flops | bytes accessed | tf_op | source)
XLA Modules:
  0.0 468.5 jit_solution(7428460371563864021)
XLA Ops:
  9.4 5.2 %all-to-all-start.1 = ((bf16[4,2,320]{2,1,0:T(2,128)(2,1)}), bf16[4,2,320]{2,1,0:T(2,128)(2,1)S(1)}, u32[]{:S(2)}, u32[]{:S(2)}) async-start(bf16[4,2,320]{2,1,0:T(2,128)(2,1)} %reshape.94), calls=%async_computation.1 | async-start | bytes 12288 | tf_op jit(solution)/shard_map/all_to_all | solution.py:70
  14.6 4.0 copy.125
  18.6 5.1 %reshape.90 = bf16[4,2,40960]{2,1,0:T(2,128)(2,1)} reshape(bf16[5120,1,2,32]{3,2,1,0:T(2,128)(2,1)} %bitcast.208) | data formatting | bytes 1310720
  23.7 4.2 all-to-all-start.3
  27.9 4.0 copy.120
  32.0 4.9 %reshape.92 = bf16[4,2,40960]{2,1,0:T(2,128)(2,1)} reshape(bf16[5120,1,2,32]{3,2,1,0:T(2,128)(2,1)} %bitcast.209) | data formatting | bytes 1310720
  37.1 4.2 all-to-all-start.2
  41.3 2.7 reshape.91
  44.0 6.2 %copy.195 = bf16[1,2,32,4,1280]{4,3,2,1,0:T(4,128)(2,1)S(1)} copy(bf16[1,2,32,4,1280]{2,1,4,3,0:T(2,128)(2,1)} %bitcast.205) | data formatting | bytes 1310720 | tf_op jit(solution)/shard_map/all_to_all | solution.py:68
  50.6 2.7 reshape.93
  53.2 6.2 %copy.194 = bf16[1,2,32,4,1280]{4,3,2,1,0:T(4,128)(2,1)S(1)} copy(bf16[1,2,32,4,1280]{2,1,4,3,0:T(2,128)(2,1)} %bitcast.206) | data formatting | bytes 1310720 | tf_op jit(solution)/shard_map/all_to_all | solution.py:69
  59.8 1.6 fusion.19
  64.2 2.2 pad_maximum_fusion
  66.4 5.4 %copy.136 = f32[30,128,256]{2,1,0:T(8,128)} copy(f32[30,128,256]{1,2,0:T(8,128)} %bitcast.203) | data formatting | bytes 7864320 | tf_op jit(solution)/shard_map/reshape | solution.py:84
  71.9 4.5 concatenate.6
  76.9 78.1 %reduce-scatter.3.cloned.1.call-done = f32[8,128,256]{2,1,0:T(8,128)} async-done(((f32[32,128,256]{2,1,0:T(8,128)}), f32[8,128,256]{2,1,0:T(8,128)}) %reduce-scatter.3.cloned.1.call-update) | async-done | bytes 1048592 | tf_op jit(solution)/shard_map/reduce_scatter | solution.py:91
  155.1 1.4 multiply_reduce_fusion.3
  156.5 2.8 fusion.28
  170.2 1.3 fusion.46
  172.2 2.0 convolution_add_fusion.5
  174.4 10.9 %all-reduce.2 = (f32[10]{0:T(128)S(1)}, f32[10]{0:T(128)S(1)}) all-reduce(f32[10]{0:T(128)S(1)} %get-tuple-element.5, f32[10]{0:T(128)S(1)} %get-tuple-element.4), channel_id=1, replica_groups=mesh['context'=4,'head'=4,'dp'=2] {'context'}, use_global_device_ids=true, to_apply=%region_2.3 | all-reduce | flops 20 | bytes 160 | tf_op jit(solution)/shard_map/psum | solution.py:85
  185.8 69.8 %all-gather.6.cloned.1.call-done = f32[32,128,256]{2,1,0:T(8,128)} async-done(((f32[8,128,256]{2,1,0:T(8,128)}), f32[32,128,256]{2,1,0:T(8,128)}) %all-gather.6.cloned.1.call-update) | async-done | bytes 4194320 | tf_op jit(solution)/shard_map/all_gather | solution.py:93
  255.6 2.4 slice.77
  258.0 1.3 fusion
  264.5 2.2 pad_maximum_fusion.1
  266.7 5.5 %copy.162 = f32[3,10,128,256]{3,2,1,0:T(8,128)} copy(f32[3,10,128,256]{2,3,1,0:T(8,128)} %pad_maximum_fusion.1) | data formatting | bytes 7864320 | tf_op jit(solution)/shard_map/stack | solution.py:47
  272.1 4.5 concatenate.7
  276.9 75.2 %reduce-scatter.5.cloned.1.call-done = f32[8,128,256]{2,1,0:T(8,128)} async-done(((f32[32,128,256]{2,1,0:T(8,128)}), f32[8,128,256]{2,1,0:T(8,128)}) %reduce-scatter.5.cloned.1.call-update) | async-done | bytes 1048592 | tf_op jit(solution)/shard_map/reduce_scatter | solution.py:91
  352.1 1.4 multiply_reduce_fusion.2
  353.5 2.9 fusion.29
  357.7 1.2 convolution_add_fusion.4
  367.4 1.4 fusion.50
  369.4 2.1 convolution_add_fusion
  371.5 4.0 copy.112
  375.6 5.0 %reshape.88 = bf16[4,2,40960]{2,1,0:T(2,128)(2,1)} reshape(bf16[5120,1,2,32]{3,2,1,0:T(2,128)(2,1)} %bitcast.210) | data formatting | bytes 1310720
  380.6 3.8 all-to-all-start
  384.4 9.6 %all-to-all-done = bf16[4,2,40960]{2,1,0:T(2,128)(2,1)S(1)} async-done(((bf16[4,2,40960]{2,1,0:T(2,128)(2,1)}), bf16[4,2,40960]{2,1,0:T(2,128)(2,1)S(1)}, u32[]{:S(2)}, u32[]{:S(2)}) %all-to-all-start) | async-done | bytes 655392 | tf_op jit(solution)/shard_map/all_to_all | solution.py:67
  393.9 2.6 reshape.89
  396.6 6.2 %copy.193 = bf16[1,2,32,4,1280]{4,3,2,1,0:T(4,128)(2,1)S(1)} copy(bf16[1,2,32,4,1280]{2,1,4,3,0:T(2,128)(2,1)} %bitcast.207) | data formatting | bytes 1310720 | tf_op jit(solution)/shard_map/all_to_all | solution.py:67
  403.3 1.4 fusion.20
  404.8 2.9 multiply_reduce_fusion.5
  407.7 2.5 convolution_bitcast_fusion.6
  410.2 3.3 multiply_reduce_fusion.4
  413.5 1.6 multiply_convert_fusion.14
  416.4 36.6 %all-gather.8.cloned.1.call-done = f32[32,128,256]{2,1,0:T(8,128)} async-done(((f32[8,128,256]{2,1,0:T(8,128)}), f32[32,128,256]{2,1,0:T(8,128)}) %all-gather.8.cloned.1.call-update) | async-done | bytes 4194320 | tf_op jit(solution)/shard_map/all_gather | solution.py:93
  452.9 2.5 slice.85
  456.2 1.7 multiply_reduce_fusion
  458.0 3.5 multiply_bitcast_fusion
  (101 shorter events, 36.9 us)
Async XLA Ops:
  7.2 7.4 %copy-start.6 = (bf16[1,2,32,5120]{3,2,1,0:T(8,128)(2,1)S(1)}, bf16[1,2,32,5120]{3,2,1,0:T(8,128)(2,1)}, u32[]{:S(2)}) copy-start(bf16[1,2,32,5120]{3,2,1,0:T(8,128)(2,1)} %param.7) | copy-start | bytes 1966084
  7.2 52.6 %all-gather.4.cloned.1.call-start = ((), (), s32[]{:S(2)}) async-start(), calls=%async_computation.6 | async-start | bytes 2949120 | tf_op jit(solution)/shard_map/all_gather | solution.py:60
  9.4 14.3 %all-to-all-start.1 = ((bf16[4,2,320]{2,1,0:T(2,128)(2,1)}), bf16[4,2,320]{2,1,0:T(2,128)(2,1)S(1)}, u32[]{:S(2)}, u32[]{:S(2)}) async-start(bf16[4,2,320]{2,1,0:T(2,128)(2,1)} %reshape.94), calls=%async_computation.1 | async-start | bytes 12288 | tf_op jit(solution)/shard_map/all_to_all | solution.py:70
  23.7 4.2 copy-start.7
  23.7 13.4 %all-to-all-start.3 = ((bf16[4,2,40960]{2,1,0:T(2,128)(2,1)}), bf16[4,2,40960]{2,1,0:T(2,128)(2,1)S(1)}, u32[]{:S(2)}, u32[]{:S(2)}) async-start(bf16[4,2,40960]{2,1,0:T(2,128)(2,1)} %reshape.90), calls=%async_computation.3 | async-start | bytes 1310720 | tf_op jit(solution)/shard_map/all_to_all | solution.py:68
  37.1 13.4 %all-to-all-start.2 = ((bf16[4,2,40960]{2,1,0:T(2,128)(2,1)}), bf16[4,2,40960]{2,1,0:T(2,128)(2,1)S(1)}, u32[]{:S(2)}, u32[]{:S(2)}) async-start(bf16[4,2,40960]{2,1,0:T(2,128)(2,1)} %reshape.92), calls=%async_computation.2 | async-start | bytes 1310720 | tf_op jit(solution)/shard_map/all_to_all | solution.py:69
  41.3 113.8 %reduce-scatter.3.cloned.1.call-start = ((), (), s32[]{:S(2)}) async-start(), calls=%async_computation.7 | async-start | bytes 5242880 | tf_op jit(solution)/shard_map/reduce_scatter | solution.py:91
  59.8 1.7 copy-start.2
  76.4 179.2 %all-gather.6.cloned.1.call-start = ((), (), s32[]{:S(2)}) async-start(), calls=%async_computation.8 | async-start | bytes 5242880 | tf_op jit(solution)/shard_map/all_gather | solution.py:93
  159.3 1.2 copy-start.4
  174.2 177.9 %reduce-scatter.5.cloned.1.call-start = ((), (), s32[]{:S(2)}) async-start(), calls=%async_computation.9 | async-start | bytes 5242880 | tf_op jit(solution)/shard_map/reduce_scatter | solution.py:91
  258.0 1.9 copy-start
  260.8 1.4 copy-start.3
  276.7 176.3 %all-gather.8.cloned.1.call-start = ((), (), s32[]{:S(2)}) async-start(), calls=%async_computation.10 | async-start | bytes 5242880 | tf_op jit(solution)/shard_map/all_gather | solution.py:93
  356.4 1.2 copy-start.5
  369.4 2.1 copy-start.8
  380.6 3.8 copy-start.9
  380.6 13.4 %all-to-all-start = ((bf16[4,2,40960]{2,1,0:T(2,128)(2,1)}), bf16[4,2,40960]{2,1,0:T(2,128)(2,1)S(1)}, u32[]{:S(2)}, u32[]{:S(2)}) async-start(bf16[4,2,40960]{2,1,0:T(2,128)(2,1)} %reshape.88), calls=%async_computation | async-start | bytes 1310720 | tf_op jit(solution)/shard_map/all_to_all | solution.py:67
  452.9 3.3 copy-start.1
Sparse Core Ops, SparseCore 0:
  9.6 13.0 all-gather.3
  76.5 78.4 reduce-scatter.2
  174.3 81.2 all-gather.5
  276.8 75.2 reduce-scatter.4
  371.6 81.2 all-gather.7
where the time goes:
time: 476 us; the launch traced here: 468 us
  waiting for transfers between devices  270 us (57%)
  local copies, waits for them, and re-layouts  85.2 us (18%)
  matrix products  51.9 us (11%)
  starting transfers between devices  18.2 us (4%)
  other arithmetic  17.4 us (4%)
  between operations  14.7 us (3%)
  blocking collectives  10.9 us (2%)
    reduce_scatter x2, waiting for transfers between devices, body(): lax.psum_scatter(flat, 'context', scatter_dimension=0, tiled=True)  153 us
    all_gather x2, waiting for transfers between devices, body(): step_all = lax.all_gather(step_own, 'context', axis=0, tiled=True)  106 us
    unnamed x34, local copies, waits for them, and re-layouts  39.7 us
    dot_general x10, matrix products, orthogonalize(): jnp.einsum('nij,nkj->nik', ortho, ortho, precision=lax.Precision.HIGHEST)  15 us
    dot_general x10, matrix products, orthogonalize(): jnp.einsum('nij,njk->nik', poly, ortho, precision=lax.Precision.HIGHEST)  12.7 us
    psum x1, blocking collectives, body(): rate_total = lax.psum(rate_part, 'context')  10.9 us
    all_to_all x1, waiting for transfers between devices, body(): lax.all_to_all(query_tok, 'head', split_axis=3, concat_axis=2, tiled=True)  9.57 us
  transfers between devices with their start and end apart: 9, of which 5 were waited for; matrix products, arithmetic and copies ran while one was open for 15% of the time, Pallas kernels for 0%

commit v1 on v0

v1 whole, which is shorter than its diff:
```python
import functools

import jax
import jax.numpy as jnp
from jax import lax
from jax.experimental import pallas as pl
from jax.experimental.pallas import tpu as pltpu
from jax.sharding import PartitionSpec as P

NS_STEPS = 5
COEFFS = (3.4445, -4.775, 2.0315)
MESH = pl.DeviceIdType.MESH
F32 = jnp.float32
BF16 = jnp.bfloat16


def dot(a, b, ca=1, cb=0):
    return lax.dot_general(a, b, (((ca,), (cb,)), ((), ())), preferred_element_type=F32)


def split(x):
    high = x.astype(BF16)
    return high, (x - high.astype(F32)).astype(BF16)


def schulz_step(ortho):
    xh, xl = split(ortho)
    both = dot(xh, jnp.concatenate([xh, xl], axis=0), 1, 1)
    half = both.shape[1] // 2
    cross = both[:, half:]
    gram = both[:, :half] + cross + cross.T
    gh, gl = split(gram)
    both = dot(gh, jnp.concatenate([gh, gl], axis=1))
    cross = both[:, half:]
    poly = COEFFS[1] * gram + COEFFS[2] * (both[:, :half] + cross + cross.T)
    ph, pl_ = split(poly)
    moved = dot(jnp.concatenate([ph, pl_], axis=1), jnp.concatenate([xh, xh], axis=0)) + dot(ph, xl)
    return COEFFS[0] * ortho + moved


def kernel(
    dims,
    q_ref, k_ref, v_ref, r_ref, w_ref, gain_ref,
    out_ref, fin_ref,
    q_buf, k_buf, v_buf, r_buf, w_buf, o_stage, f_stage,
    w_now, w_bf, g_acc,
    tok_send, tok_recv, r_send, r_recv, w_send, w_recv, out_send, out_recv, fin_send, fin_recv,
):
    contexts, groups, heads, blocks, rows, dh, hf = dims
    peers = contexts * groups
    tokens = peers * rows
    local_tokens = groups * rows
    ctx, grp, core = lax.axis_index("context"), lax.axis_index("head"), lax.axis_index("dp")
    me = ctx * groups + grp

    def first_head(c):
        return (c * heads) // contexts

    own_first = first_head(ctx)
    own_count = first_head(ctx + 1) - own_first
    most = -(-heads // contexts)

    barrier = pltpu.get_barrier_semaphore()

    def greet(i, carry):
        peer = (me + i) % peers
        pl.semaphore_signal(barrier, inc=1, device_id=(peer // groups, peer % groups, core), device_id_type=MESH)
        return carry

    lax.fori_loop(1, peers, greet, 0)
    pl.semaphore_signal(barrier, inc=1, device_id=(ctx, grp, 1 - core), device_id_type=MESH)
    pl.semaphore_wait(barrier, peers)

    my_rows = pl.ds(pl.multiple_of(core * (dh // 2), dh // 2), dh // 2)
    w_src = w_ref.at[:, pl.ds(jnp.minimum(own_first, heads - most), most)]
    w_dst = w_buf.at[:, :, my_rows, :]
    w_remote = pltpu.make_async_remote_copy(
        w_src, w_dst, w_send, w_recv, device_id=(ctx, grp, 1 - core), device_id_type=MESH
    )
    w_remote.start()
    pltpu.make_async_copy(w_src, w_dst, w_recv).start()

    my_tokens = pl.ds(pl.multiple_of(me * rows, rows), rows)
    r_dst = r_buf.at[:, my_tokens, :]
    pltpu.make_async_copy(r_ref.at[0], r_dst, r_recv).start()

    def send_rates(i, carry):
        peer = (me + i) % peers
        pltpu.make_async_remote_copy(
            r_ref.at[0], r_dst, r_send, r_recv,
            device_id=(peer // groups, peer % groups, core), device_id_type=MESH,
        ).start()
        return carry

    lax.fori_loop(1, peers, send_rates, 0)

    arrays = ((k_ref, k_buf), (v_ref, v_buf), (q_ref, q_buf))

    def columns_of(c, g, j):
        return pl.ds(pl.multiple_of((g * heads + first_head(c) + j) * dh, dh), dh)

    def send_head(j, carry):
        for which in ((0, 1), (2,)):
            @pl.when(j < own_count)
            def _():
                for a in which:
                    src, buf = arrays[a]
                    pltpu.make_async_copy(
                        src.at[0, :, :, columns_of(ctx, grp, j)], buf.at[j, :, my_tokens, :], tok_recv.at[a, j]
                    ).start()

            def send_to(i, inner):
                peer = (me + i) % peers
                c, g = peer // groups, peer % groups

                @pl.when(j < first_head(c + 1) - first_head(c))
                def _():
                    for a in which:
                        src, buf = arrays[a]
                        pltpu.make_async_remote_copy(
                            src.at[0, :, :, columns_of(c, g, j)], buf.at[j, :, my_tokens, :],
                            tok_send.at[a], tok_recv.at[a, j],
                            device_id=(c, g, core), device_id_type=MESH,
                        ).start()

                return inner

            lax.fori_loop(1, peers, send_to, 0)
        return carry

    lax.fori_loop(0, most, send_head, 0)

    def wait_for(ref, sem):
        pltpu.make_async_copy(ref, ref, sem).wait()

    wait_for(w_buf, w_recv)
    wait_for(r_buf, r_recv)

    chunk = min(tokens, 512)
    chunks = tokens // chunk

    def work(j, carry):
        shift = own_first - jnp.minimum(own_first, heads - most)
        lane = grp * heads + own_first + j
        init_sq = []
        for m in range(3):
            start = w_buf[m, shift + j].astype(F32)
            w_now[m] = start
            init_sq.append(jnp.sqrt(jnp.sum(start * start, axis=0, keepdims=True)))
        wait_for(k_buf.at[j], tok_recv.at[0, j])
        wait_for(v_buf.at[j], tok_recv.at[1, j])

        def block(b, norms):
            for m in range(3):
                w_bf[b, m] = w_now[m].astype(BF16)
                g_acc[m] = jnp.zeros((dh, hf), F32)

            def part(i, total):
                at = pl.ds(pl.multiple_of(i * chunk, chunk), chunk)
                keys, vals = k_buf[j, b, at, :], v_buf[j, b, at, :]
                rate_all = r_buf[b, at, :].astype(F32)
                lanes = lax.broadcasted_iota(jnp.int32, rate_all.shape, 1)
                rate = jnp.sum(jnp.where(lanes == lane, rate_all, 0.0), axis=1, keepdims=True)
                gate = dot(keys, w_bf[b, 0])
                up = dot(keys, w_bf[b, 1])
                back = dot(vals, w_bf[b, 2]) * rate
                sigma = jax.nn.sigmoid(gate)
                act = gate * sigma
                hidden = (act * up).astype(BF16)
                d_up = (back * act).astype(BF16)
                d_gate = (back * up * (sigma * (1.0 + gate * (1.0 - sigma)))).astype(BF16)
                rated = (vals.astype(F32) * rate).astype(BF16)
                g_acc[0] += dot(keys, d_gate, 0, 0)
                g_acc[1] += dot(keys, d_up, 0, 0)
                g_acc[2] += dot(rated, hidden, 0, 0)
                return total + jnp.sum(rate, axis=0, keepdims=True)

            eta = lax.fori_loop(0, chunks, part, jnp.zeros((1, 1), F32)) / tokens
            ortho = []
            for m in range(3):
                grad = g_acc[m]
                frob = jnp.sqrt(jnp.sum(jnp.sum(grad * grad, axis=0, keepdims=True), axis=1, keepdims=True)) + 1e-07
                ortho.append(grad / frob)
            ortho = lax.fori_loop(0, NS_STEPS, lambda s, xs: tuple(schulz_step(x) for x in xs), tuple(ortho))
            for m in range(3):
                moved = w_now[m] + eta * ortho[m]
                scale = norms[m] * lax.rsqrt(jnp.sum(moved * moved, axis=0, keepdims=True) + 1e-06)
                w_now[m] = moved * scale
            return norms

        lax.fori_loop(0, blocks, block, tuple(init_sq))

        for m in range(3):
            f_stage[j, m] = w_now[m].astype(BF16)
        head = own_first + j
        fin_dst = fin_ref.at[:, head]
        pltpu.make_async_copy(f_stage.at[j], fin_dst, fin_recv).start()

        def send_final(i, inner):
            pltpu.make_async_remote_copy(
                f_stage.at[j], fin_dst, fin_send.at[j, i], fin_recv,
                device_id=((ctx + i) % contexts, grp, core), device_id_type=MESH,
            ).start()
            return inner

        lax.fori_loop(1, contexts, send_final, 0)

        wait_for(q_buf.at[j], tok_recv.at[2, j])
        gain = gain_ref[head]

        def answer(b, inner):
            def part(i, innermost):
                at = pl.ds(pl.multiple_of(i * chunk, chunk), chunk)
                queries = q_buf[j, b, at, :]
                gate = dot(queries, w_bf[b, 0])
                up = dot(queries, w_bf[b, 1])
                hidden = (gate * jax.nn.sigmoid(gate) * up).astype(BF16)
                mapped = dot(hidden, w_bf[b, 2], 1, 1)
                mean_sq = jnp.mean(mapped * mapped, axis=1, keepdims=True)
                o_stage[j, b, at, :] = (mapped * lax.rsqrt(mean_sq + 1e-06) * gain).astype(BF16)
                return innermost

            lax.fori_loop(0, chunks, part, 0)
            return inner

        lax.fori_loop(0, blocks, answer, 0)

        out_dst = out_ref.at[0, :, :, pl.ds(pl.multiple_of(head * dh, dh), dh)]

        def of_context(c):
            return o_stage.at[j, :, pl.ds(pl.multiple_of(c * local_tokens, local_tokens), local_tokens), :]

        pltpu.make_async_copy(of_context(ctx), out_dst, out_recv).start()

        def send_out(i, inner):
            c = (ctx + i) % contexts
            pltpu.make_async_remote_copy(
                of_context(c), out_dst, out_send.at[j, i], out_recv,
                device_id=(c, grp, core), device_id_type=MESH,
            ).start()
            return inner

        lax.fori_loop(1, contexts, send_out, 0)
        return carry

    lax.fori_loop(0, own_count, work, 0)

    w_remote.wait_send()
    wait_for(r_buf.at[:, 0:tokens - rows, :], r_send)
    for count in sorted({heads // contexts, most}):
        @pl.when(own_count == count)
        def _():
            for a in range(3):
                src = arrays[a][0]
                wait_for(src.at[0, :, :, 0:(groups * heads - count) * dh], tok_send.at[a])

    def sent(j, carry):
        def one(i, inner):
            wait_for(f_stage.at[j], fin_send.at[j, i])
            wait_for(o_stage.at[j, :, 0:local_tokens, :], out_send.at[j, i])
            return inner

        return lax.fori_loop(1, contexts, one, carry)

    lax.fori_loop(0, own_count, sent, 0)
    wait_for(out_ref, out_recv)
    wait_for(fin_ref, fin_recv)


def body(contexts, groups, query_tok, key_tok, value_tok, token_rates, fast_init, out_gain):
    _, blocks, rows, _ = query_tok.shape
    _, heads, half, hf = fast_init.shape
    dh = 2 * half
    peers = contexts * groups
    tokens = peers * rows
    most = -(-heads // contexts)
    rates = jnp.pad(token_rates, ((0, 0), (0, 0), (0, 0), (0, 128 - token_rates.shape[3])))
    gain = out_gain.astype(F32).reshape(heads, 1, dh)
    dims = (contexts, groups, heads, blocks, rows, dh, hf)
    anywhere = pl.BlockSpec(memory_space=pl.ANY)
    tok = pltpu.VMEM((most, blocks, tokens, dh), BF16)
    dma = pltpu.SemaphoreType.DMA
    head_out, final = pl.pallas_call(
        functools.partial(kernel, dims),
        out_shape=(
            jax.ShapeDtypeStruct((1, blocks, groups * rows, heads * dh), BF16),
            jax.ShapeDtypeStruct((3, heads, dh, hf), BF16),
        ),
        in_specs=[anywhere] * 5 + [pl.BlockSpec(memory_space=pltpu.VMEM)],
        out_specs=(anywhere, anywhere),
        scratch_shapes=[
            tok, tok, tok,
            pltpu.VMEM((blocks, tokens, 128), BF16),
            pltpu.VMEM((3, most, dh, hf), BF16),
            tok,
            pltpu.VMEM((most, 3, dh, hf), BF16),
            pltpu.VMEM((3, dh, hf), F32),
            pltpu.VMEM((blocks, 3, dh, hf), BF16),
            pltpu.VMEM((3, dh, hf), F32),
            dma((3,)), dma((3, most)), dma, dma, dma, dma,
            dma((most, contexts)), dma, dma((most, contexts)), dma,
        ],
        compiler_params=pltpu.CompilerParams(
            collective_id=0, has_side_effects=True, vmem_limit_bytes=48 * 1024 * 1024
        ),
    )(query_tok, key_tok, value_tok, rates, fast_init, gain)
    return head_out, final.astype(F32)[None]


def solution(mesh):
    return jax.shard_map(
        functools.partial(body, mesh.shape["context"], mesh.shape["head"]),
        mesh=mesh,
        in_specs=(
            P("dp", None, ("context", "head"), None),
            P("dp", None, ("context", "head"), None),
            P("dp", None, ("context", "head"), None),
            P("dp", None, ("context", "head"), None),
            P(None, "head", "dp", None),
            P("head"),
        ),
        out_specs=(P("dp", None, "context", "head"), P("dp", None, "head", None, None)),
        check_vma=False,
    )
```

time: 476 us -> 121 us (0.25); the launches traced: 468 us -> 121 us
  waiting for transfers between devices: 270 us -> 0 us
  Pallas kernels: 0 us -> 111 us
  local copies, waits for them, and re-layouts: 85.2 us -> 6.72 us
  matrix products: 51.9 us -> 0 us
  starting transfers between devices: 18.2 us -> 0 us
  other arithmetic: 17.4 us -> 2.41 us
  between operations: 14.7 us -> 0.64 us
  blocking collectives: 10.9 us -> 0 us
    reduce_scatter x2 -> x0, waiting for transfers between devices: 153 us -> none  [body(): lax.psum_scatter(flat, 'context', scatter_dimension=0, tiled=True)]
    pallas_call x0 -> x1, Pallas kernels: none -> 111 us  [body(): pl.pallas_call(functools.partial(kernel, dims), out_shape=(jax.ShapeDtype...]
    all_gather x3 -> x0, waiting for transfers between devices: 106 us -> none  [the longest x2 106 us: body(): step_all = lax.all_gather(step_own, 'context', axis=0, tiled=True)]
    dot_general x46 -> x0, matrix products: 51.9 us -> none  [the longest x10 15 us: orthogonalize(): jnp.einsum('nij,nkj->nik', ortho, ortho, precision=lax.Precision.HIGHEST)]
    unnamed x34 -> x9, local copies, waits for them, and re-layouts: 39.7 us -> 5.3 us
    all_to_all x8 -> x0, local copies, waits for them, and re-layouts: 18.9 us -> none  [the longest x2 6.26 us: body(): lax.all_to_all(query_tok, 'head', split_axis=3, concat_axis=2, tiled=True)]
    all_to_all x4 -> x0, starting transfers between devices: 17.4 us -> none  [the longest x1 5.16 us: body(): lax.all_to_all(token_rates, 'head', split_axis=3, concat_axis=2, tiled=True)]
    psum x1 -> x0, blocking collectives: 10.9 us -> none  [body(): rate_total = lax.psum(rate_part, 'context')]
  transfers between devices with their start and end apart: 9 -> 0, of which waited for: 5 -> 0; matrix products, arithmetic and copies ran while one was open for 15% -> 0% of each run, Pallas kernels for 0% -> 0%
where the time goes in v1:
time: 121 us
  Pallas kernels  111 us (92%)
  local copies, waits for them, and re-layouts  6.72 us (6%)
  other arithmetic  2.41 us (2%)
    pallas_call x1, Pallas kernels, body(): pl.pallas_call(functools.partial(kernel, dims), out_shape=(jax.ShapeDtype...  111 us
    unnamed x9, local copies, waits for them, and re-layouts  5.3 us

profile of v1, /device:TPU:0, one launch (start us, length us, event | category | flops | bytes accessed | tf_op | source)
XLA Modules:
  0.0 120.9 jit_solution(16551205918756991265)
XLA Ops:
  0.6 0.7 reshape.12.gain_ref
  1.3 0.7 pad.4.r_ref
  2.1 0.0 copy-start
  2.1 1.2 copy-done
  3.3 0.0 copy-start.1
  3.3 1.1 copy-done.1
  4.3 0.0 copy-start.2
  4.3 1.1 copy-done.2
  5.4 0.0 copy-start.3
  5.4 1.1 copy-done.3
  6.5 111.1 %shard_map.77 = (bf16[1,2,128,1280]{3,2,1,0:T(8,128)(2,1)S(1)}, bf16[3,10,128,256]{3,2,1,0:T(8,128)(2,1)S(1)}) custom-call(bf16[1,2,32,5120]{3,2,1,0:T(8,128)(2,1)S(1)} %copy-done.1, bf16[1,2,32,5120]{3,2,1,0:T(8,128)(2,1)S(1)} %copy-done.2, bf16[1,2,32,5120]{3,2,1,0:T(8,128)(2,1)S(1)} %copy-done.3, bf16[1,2,32,128]{3,2,1,0:T(8,128)(2,1)S(1)} %pad.4.r_ref, ...), custom_call_target="tpu_custom_call" | custom-call | tf_op jit(solution)/shard_map/pallas_call | solution.py:283
  117.7 2.4 %bitcast_convert_fusion = f32[1,3,10,128,256]{4,3,2,1,0:T(8,128)} fusion(bf16[3,10,128,256]{3,2,1,0:T(8,128)(2,1)S(1)} %get-tuple-element.5), kind=kLoop, calls=%fused_computation | loop fusion | flops 983040 | bytes 5898240 | tf_op jit(solution)/shard_map/broadcast_in_dim | solution.py:307
  120.1 0.8 copy.9
Async XLA Ops:
  2.1 1.2 copy-start
  3.3 1.1 copy-start.1
  4.3 1.1 copy-start.2
  5.4 1.1 copy-start.3

commit v2 on v1

--- a/solution.py
+++ b/solution.py
@@ -42,9 +42,10 @@
     dims,
     q_ref, k_ref, v_ref, r_ref, w_ref, gain_ref,
     out_ref, fin_ref,
-    q_buf, k_buf, v_buf, r_buf, w_buf, o_stage, f_stage,
+    q_buf, k_buf, v_buf, r_buf, w_buf, first_buf, first_out, o_stage, f_stage,
     w_now, w_bf, g_acc,
-    tok_send, tok_recv, r_send, r_recv, w_send, w_recv, out_send, out_recv, fin_send, fin_recv,
+    tok_send, tok_recv, first_send, first_recv, r_send, r_recv, w_send, w_recv,
+    out_send, out_recv, fin_send, fin_recv,
 ):
     contexts, groups, heads, blocks, rows, dh, hf = dims
     peers = contexts * groups
@@ -72,7 +73,7 @@
     pl.semaphore_wait(barrier, peers)
 
     my_rows = pl.ds(pl.multiple_of(core * (dh // 2), dh // 2), dh // 2)
-    w_src = w_ref.at[:, pl.ds(jnp.minimum(own_first, heads - most), most)]
+    w_src = w_ref
     w_dst = w_buf.at[:, :, my_rows, :]
     w_remote = pltpu.make_async_remote_copy(
         w_src, w_dst, w_send, w_recv, device_id=(ctx, grp, 1 - core), device_id_type=MESH
@@ -94,7 +95,28 @@
 
     lax.fori_loop(1, peers, send_rates, 0)
 
-    arrays = ((k_ref, k_buf), (v_ref, v_buf), (q_ref, q_buf))
+    later = blocks - 1
+    arrays = ((k_ref, k_buf, blocks), (v_ref, v_buf, blocks), (q_ref, q_buf, later))
+
+    def tokens_of(a, where):
+        src, _, count = arrays[a]
+        return src.at[0, pl.ds(blocks - count, count), :, where]
+
+    def first_columns(g):
+        return pl.ds(pl.multiple_of(g * heads * dh, heads * dh), heads * dh)
+
+    first_dst = first_buf.at[pl.ds(pl.multiple_of(grp * rows, rows), rows), :]
+
+    def send_first(i, carry):
+        g = (grp + i) % groups
+        pltpu.make_async_remote_copy(
+            q_ref.at[0, 0, :, first_columns(g)], first_dst, first_send.at[i], first_recv,
+            device_id=(ctx, g, core), device_id_type=MESH,
+        ).start()
+        return carry
+
+    pltpu.make_async_copy(q_ref.at[0, 0, :, first_columns(grp)], first_dst, first_recv).start()
+    lax.fori_loop(1, groups, send_first, 0)
 
     def columns_of(c, g, j):
         return pl.ds(pl.multiple_of((g * heads + first_head(c) + j) * dh, dh), dh)
@@ -104,9 +126,9 @@
             @pl.when(j < own_count)
             def _():
                 for a in which:
-                    src, buf = arrays[a]
+                    buf = arrays[a][1]
                     pltpu.make_async_copy(
-                        src.at[0, :, :, columns_of(ctx, grp, j)], buf.at[j, :, my_tokens, :], tok_recv.at[a, j]
+                        tokens_of(a, columns_of(ctx, grp, j)), buf.at[j, :, my_tokens, :], tok_recv.at[a, j]
                     ).start()
 
             def send_to(i, inner):
@@ -116,9 +138,9 @@
                 @pl.when(j < first_head(c + 1) - first_head(c))
                 def _():
                     for a in which:
-                        src, buf = arrays[a]
+                        buf = arrays[a][1]
                         pltpu.make_async_remote_copy(
-                            src.at[0, :, :, columns_of(c, g, j)], buf.at[j, :, my_tokens, :],
+                            tokens_of(a, columns_of(c, g, j)), buf.at[j, :, my_tokens, :],
                             tok_send.at[a], tok_recv.at[a, j],
                             device_id=(c, g, core), device_id_type=MESH,
                         ).start()
@@ -133,18 +155,57 @@
     def wait_for(ref, sem):
         pltpu.make_async_copy(ref, ref, sem).wait()
 
+    def answer(queries, weights, gain):
+        gate = dot(queries, weights[0])
+        up = dot(queries, weights[1])
+        hidden = (gate * jax.nn.sigmoid(gate) * up).astype(BF16)
+        mapped = dot(hidden, weights[2], 1, 1)
+        mean_sq = jnp.mean(mapped * mapped, axis=1, keepdims=True)
+        return (mapped * lax.rsqrt(mean_sq + 1e-06) * gain).astype(BF16)
+
     wait_for(w_buf, w_recv)
+    wait_for(first_buf, first_recv)
+
+    def answer_first(h, carry):
+        at = pl.ds(pl.multiple_of(h * dh, dh), dh)
+        first_out[:, at] = answer(first_buf[:, at], [w_buf[m, h] for m in range(3)], gain_ref[h])
+        return carry
+
+    lax.fori_loop(0, heads, answer_first, 0)
+    first_copy = pltpu.make_async_copy(first_out, out_ref.at[0, 0], first_send.at[0])
+    first_copy.start()
     wait_for(r_buf, r_recv)
+
+    def send_final(head, side, src):
+        return pltpu.make_async_remote_copy(
+            src, fin_ref.at[:, head], fin_send.at[head, side], fin_recv.at[head],
+            device_id=(ctx + (1 if side else -1), grp, core), device_id_type=MESH,
+        )
+
+    def relay(step):
+        for far in range(1, contexts - 1):
+            slot = step - far
+            for side in (0, 1):
+                owner = ctx - far if side else ctx + far
+                exists = (owner >= 0) & (owner < contexts)
+                passes = (ctx < contexts - 1) if side else (ctx > 0)
+                count = first_head(owner + 1) - first_head(owner)
+
+                @pl.when(exists & passes & (slot >= 0) & (slot < count))
+                def _():
+                    head = first_head(owner) + slot
+                    wait_for(fin_ref.at[:, head], fin_recv.at[head])
+                    send_final(head, side, fin_ref.at[:, head]).start()
 
     chunk = min(tokens, 512)
     chunks = tokens // chunk
 
     def work(j, carry):
-        shift = own_first - jnp.minimum(own_first, heads - most)
-        lane = grp * heads + own_first + j
+        head = own_first + j
+        lane = grp * heads + head
         init_sq = []
         for m in range(3):
-            start = w_buf[m, shift + j].astype(F32)
+            start = w_buf[m, head].astype(F32)
             w_now[m] = start
             init_sq.append(jnp.sqrt(jnp.sum(start * start, axis=0, keepdims=True)))
         wait_for(k_buf.at[j], tok_recv.at[0, j])
@@ -192,40 +253,28 @@
 
         for m in range(3):
             f_stage[j, m] = w_now[m].astype(BF16)
-        head = own_first + j
-        fin_dst = fin_ref.at[:, head]
-        pltpu.make_async_copy(f_stage.at[j], fin_dst, fin_recv).start()
-
-        def send_final(i, inner):
-            pltpu.make_async_remote_copy(
-                f_stage.at[j], fin_dst, fin_send.at[j, i], fin_recv,
-                device_id=((ctx + i) % contexts, grp, core), device_id_type=MESH,
-            ).start()
-            return inner
-
-        lax.fori_loop(1, contexts, send_final, 0)
-
+        pltpu.make_async_copy(f_stage.at[j], fin_ref.at[:, head], fin_recv.at[head]).start()
+        for side in (0, 1):
+            @pl.when((ctx < contexts - 1) if side else (ctx > 0))
+            def _():
+                send_final(head, side, f_stage.at[j]).start()
+
+        relay(j)
         wait_for(q_buf.at[j], tok_recv.at[2, j])
         gain = gain_ref[head]
 
-        def answer(b, inner):
+        def answer_later(b, inner):
             def part(i, innermost):
                 at = pl.ds(pl.multiple_of(i * chunk, chunk), chunk)
-                queries = q_buf[j, b, at, :]
-                gate = dot(queries, w_bf[b, 0])
-                up = dot(queries, w_bf[b, 1])
-                hidden = (gate * jax.nn.sigmoid(gate) * up).astype(BF16)
-                mapped = dot(hidden, w_bf[b, 2], 1, 1)
-                mean_sq = jnp.mean(mapped * mapped, axis=1, keepdims=True)
-                o_stage[j, b, at, :] = (mapped * lax.rsqrt(mean_sq + 1e-06) * gain).astype(BF16)
+                o_stage[j, b, at, :] = answer(q_buf[j, b, at, :], [w_bf[b + 1, m] for m in range(3)], gain)
                 return innermost
 
             lax.fori_loop(0, chunks, part, 0)
             return inner
 
-        lax.fori_loop(0, blocks, answer, 0)
-
-        out_dst = out_ref.at[0, :, :, pl.ds(pl.multiple_of(head * dh, dh), dh)]
+        lax.fori_loop(0, later, answer_later, 0)
+
+        out_dst = out_ref.at[0, pl.ds(1, later), :, pl.ds(pl.multiple_of(head * dh, dh), dh)]
 
         def of_context(c):
             return o_stage.at[j, :, pl.ds(pl.multiple_of(c * local_tokens, local_tokens), local_tokens), :]
@@ -245,26 +294,56 @@
 
     lax.fori_loop(0, own_count, work, 0)
 
+    def relay_rest(step, carry):
+        relay(step)
+        return carry
+
+    lax.fori_loop(own_count, most + contexts, relay_rest, 0)
+
     w_remote.wait_send()
     wait_for(r_buf.at[:, 0:tokens - rows, :], r_send)
     for count in sorted({heads // contexts, most}):
         @pl.when(own_count == count)
         def _():
             for a in range(3):
-                src = arrays[a][0]
-                wait_for(src.at[0, :, :, 0:(groups * heads - count) * dh], tok_send.at[a])
-
-    def sent(j, carry):
+                wait_for(tokens_of(a, pl.ds(0, (groups * heads - count) * dh)), tok_send.at[a])
+
+    first_copy.wait()
+
+    def first_sent(i, carry):
+        wait_for(first_dst, first_send.at[i])
+        return carry
+
+    lax.fori_loop(1, groups, first_sent, 0)
+
+    def outs_sent(j, carry):
         def one(i, inner):
-            wait_for(f_stage.at[j], fin_send.at[j, i])
             wait_for(o_stage.at[j, :, 0:local_tokens, :], out_send.at[j, i])
             return inner
 
         return lax.fori_loop(1, contexts, one, carry)
 
-    lax.fori_loop(0, own_count, sent, 0)
-    wait_for(out_ref, out_recv)
-    wait_for(fin_ref, fin_recv)
+    lax.fori_loop(0, own_count, outs_sent, 0)
+
+    def final_done(head, carry):
+        from_left = head < own_first
+        from_right = head >= own_first + own_count
+        to_right, to_left = ctx < contexts - 1, ctx > 0
+        went = (to_left & ~from_left, to_right & ~from_right)
+        passed = (from_left & to_right) | (from_right & to_left)
+        for side in (0, 1):
+            @pl.when(went[side])
+            def _():
+                send_final(head, side, fin_ref.at[:, head]).wait_send()
+
+        @pl.when(~passed)
+        def _():
+            wait_for(fin_ref.at[:, head], fin_recv.at[head])
+
+        return carry
+
+    lax.fori_loop(0, heads, final_done, 0)
+    wait_for(out_ref.at[0, pl.ds(1, later)], out_recv)
 
 
 def body(contexts, groups, query_tok, key_tok, value_tok, token_rates, fast_init, out_gain):
@@ -279,6 +358,8 @@
     dims = (contexts, groups, heads, blocks, rows, dh, hf)
     anywhere = pl.BlockSpec(memory_space=pl.ANY)
     tok = pltpu.VMEM((most, blocks, tokens, dh), BF16)
+    later_tok = pltpu.VMEM((most, blocks - 1, tokens, dh), BF16)
+    first_tok = pltpu.VMEM((groups * rows, heads * dh), BF16)
     dma = pltpu.SemaphoreType.DMA
     head_out, final = pl.pallas_call(
         functools.partial(kernel, dims),
@@ -289,16 +370,17 @@
         in_specs=[anywhere] * 5 + [pl.BlockSpec(memory_space=pltpu.VMEM)],
         out_specs=(anywhere, anywhere),
         scratch_shapes=[
-            tok, tok, tok,
+            later_tok, tok, tok,
             pltpu.VMEM((blocks, tokens, 128), BF16),
-            pltpu.VMEM((3, most, dh, hf), BF16),
-            tok,
+            pltpu.VMEM((3, heads, dh, hf), BF16),
+            first_tok, first_tok,
+            later_tok,
             pltpu.VMEM((most, 3, dh, hf), BF16),
             pltpu.VMEM((3, dh, hf), F32),
             pltpu.VMEM((blocks, 3, dh, hf), BF16),
             pltpu.VMEM((3, dh, hf), F32),
-            dma((3,)), dma((3, most)), dma, dma, dma, dma,
-            dma((most, contexts)), dma, dma((most, contexts)), dma,
+            dma((3,)), dma((3, most)), dma((groups,)), dma, dma, dma, dma, dma,
+            dma((most, contexts)), dma, dma((heads, 2)), dma((heads,)),
         ],
         compiler_params=pltpu.CompilerParams(
             collective_id=0, has_side_effects=True, vmem_limit_bytes=48 * 1024 * 1024

time: 121 us -> 110 us (0.909)
  the two profiles are of different devices: /device:TPU:0 before, /device:TPU:6 now
where the time goes in v2:
time: 110 us
  Pallas kernels  100 us (91%)
  local copies, waits for them, and re-layouts  6.72 us (6%)
  other arithmetic  2.41 us (2%)
    pallas_call x1, Pallas kernels, body(): pl.pallas_call(functools.partial(kernel, dims), out_shape=(jax.ShapeDtype...  100 us
    unnamed x9, local copies, waits for them, and re-layouts  5.3 us
    broadcast_in_dim x1, other arithmetic, body(): return (head_out, final.astype(F32)[None])  2.41 us

profile of v2, /device:TPU:6, one launch (start us, length us, event | category | flops | bytes accessed | tf_op | source)
XLA Modules:
  0.0 109.8 jit_solution(11846060553800994350)
XLA Ops:
  0.6 0.7 reshape.12.gain_ref
  1.3 0.7 pad.4.r_ref
  2.1 0.0 copy-start
  2.1 1.2 %copy-done = bf16[3,10,64,256]{3,2,1,0:T(8,128)(2,1)S(1)} copy-done((bf16[3,10,64,256]{3,2,1,0:T(8,128)(2,1)S(1)}, bf16[3,10,64,256]{3,2,1,0:T(8,128)(2,1)}, u32[]{:S(2)}) %copy-start) | copy-done | bytes 983064
  3.3 0.0 copy-start.1
  3.3 1.1 copy-done.1
  4.3 0.0 copy-start.2
  4.3 1.1 copy-done.2
  5.4 0.0 copy-start.3
  5.4 1.1 copy-done.3
  6.5 100.0 %shard_map.77 = (bf16[1,2,128,1280]{3,2,1,0:T(8,128)(2,1)S(1)}, bf16[3,10,128,256]{3,2,1,0:T(8,128)(2,1)S(1)}) custom-call(bf16[1,2,32,5120]{3,2,1,0:T(8,128)(2,1)S(1)} %copy-done.1, bf16[1,2,32,5120]{3,2,1,0:T(8,128)(2,1)S(1)} %copy-done.2, bf16[1,2,32,5120]{3,2,1,0:T(8,128)(2,1)S(1)} %copy-done.3, bf16[1,2,32,128]{3,2,1,0:T(8,128)(2,1)S(1)} %pad.4.r_ref, ...), custom_call_target="tpu_custom_call" | custom-call | tf_op jit(solution)/shard_map/pallas_call | solution.py:364
  106.5 2.4 %bitcast_convert_fusion = f32[1,3,10,128,256]{4,3,2,1,0:T(8,128)} fusion(bf16[3,10,128,256]{3,2,1,0:T(8,128)(2,1)S(1)} %get-tuple-element.5), kind=kLoop, calls=%fused_computation | loop fusion | flops 983040 | bytes 5898240 | tf_op jit(solution)/shard_map/broadcast_in_dim | solution.py:389
  109.0 0.8 copy.9
Async XLA Ops:
  2.1 1.2 %copy-start = (bf16[3,10,64,256]{3,2,1,0:T(8,128)(2,1)S(1)}, bf16[3,10,64,256]{3,2,1,0:T(8,128)(2,1)}, u32[]{:S(2)}) copy-start(bf16[3,10,64,256]{3,2,1,0:T(8,128)(2,1)} %w_ref.1) | copy-start | bytes 2949124
  3.3 1.1 copy-start.1
  4.3 1.1 copy-start.2
  5.4 1.1 copy-start.3

commit v3 on v2

--- a/solution.py
+++ b/solution.py
@@ -82,13 +82,13 @@
     pltpu.make_async_copy(w_src, w_dst, w_recv).start()
 
     my_tokens = pl.ds(pl.multiple_of(me * rows, rows), rows)
-    r_dst = r_buf.at[:, my_tokens, :]
-    pltpu.make_async_copy(r_ref.at[0], r_dst, r_recv).start()
+    r_dst = r_buf.at[my_tokens, :]
+    pltpu.make_async_copy(r_ref, r_dst, r_recv).start()
 
     def send_rates(i, carry):
         peer = (me + i) % peers
         pltpu.make_async_remote_copy(
-            r_ref.at[0], r_dst, r_send, r_recv,
+            r_ref, r_dst, r_send, r_recv,
             device_id=(peer // groups, peer % groups, core), device_id_type=MESH,
         ).start()
         return carry
@@ -114,9 +114,6 @@
             device_id=(ctx, g, core), device_id_type=MESH,
         ).start()
         return carry
-
-    pltpu.make_async_copy(q_ref.at[0, 0, :, first_columns(grp)], first_dst, first_recv).start()
-    lax.fori_loop(1, groups, send_first, 0)
 
     def columns_of(c, g, j):
         return pl.ds(pl.multiple_of((g * heads + first_head(c) + j) * dh, dh), dh)
@@ -150,7 +147,9 @@
             lax.fori_loop(1, peers, send_to, 0)
         return carry
 
-    lax.fori_loop(0, most, send_head, 0)
+    lax.fori_loop(0, 1, send_head, 0)
+    pltpu.make_async_copy(q_ref.at[0, 0, :, first_columns(grp)], first_dst, first_recv).start()
+    lax.fori_loop(1, groups, send_first, 0)
 
     def wait_for(ref, sem):
         pltpu.make_async_copy(ref, ref, sem).wait()
@@ -172,6 +171,7 @@
         return carry
 
     lax.fori_loop(0, heads, answer_first, 0)
+    lax.fori_loop(1, most, send_head, 0)
     first_copy = pltpu.make_async_copy(first_out, out_ref.at[0, 0], first_send.at[0])
     first_copy.start()
     wait_for(r_buf, r_recv)
@@ -182,9 +182,9 @@
             device_id=(ctx + (1 if side else -1), grp, core), device_id_type=MESH,
         )
 
-    def relay(step):
-        for far in range(1, contexts - 1):
-            slot = step - far
+    def relay(step, low, high):
+        for far in range(low, high):
+            slot = step - max(far - 1, 1)
             for side in (0, 1):
                 owner = ctx - far if side else ctx + far
                 exists = (owner >= 0) & (owner < contexts)
@@ -212,6 +212,10 @@
         wait_for(v_buf.at[j], tok_recv.at[1, j])
 
         def block(b, norms):
+            @pl.when(b == blocks - 1)
+            def _():
+                relay(j, 1, min(2, contexts - 1))
+
             for m in range(3):
                 w_bf[b, m] = w_now[m].astype(BF16)
                 g_acc[m] = jnp.zeros((dh, hf), F32)
@@ -219,9 +223,9 @@
             def part(i, total):
                 at = pl.ds(pl.multiple_of(i * chunk, chunk), chunk)
                 keys, vals = k_buf[j, b, at, :], v_buf[j, b, at, :]
-                rate_all = r_buf[b, at, :].astype(F32)
+                rate_all = r_buf[at, :].astype(F32)
                 lanes = lax.broadcasted_iota(jnp.int32, rate_all.shape, 1)
-                rate = jnp.sum(jnp.where(lanes == lane, rate_all, 0.0), axis=1, keepdims=True)
+                rate = jnp.sum(jnp.where(lanes == lane + b * (groups * heads), rate_all, 0.0), axis=1, keepdims=True)
                 gate = dot(keys, w_bf[b, 0])
                 up = dot(keys, w_bf[b, 1])
                 back = dot(vals, w_bf[b, 2]) * rate
@@ -259,7 +263,7 @@
             def _():
                 send_final(head, side, f_stage.at[j]).start()
 
-        relay(j)
+        relay(j, 2, contexts - 1)
         wait_for(q_buf.at[j], tok_recv.at[2, j])
         gain = gain_ref[head]
 
@@ -295,13 +299,13 @@
     lax.fori_loop(0, own_count, work, 0)
 
     def relay_rest(step, carry):
-        relay(step)
+        relay(step, 1, contexts - 1)
         return carry
 
     lax.fori_loop(own_count, most + contexts, relay_rest, 0)
 
     w_remote.wait_send()
-    wait_for(r_buf.at[:, 0:tokens - rows, :], r_send)
+    wait_for(r_buf.at[0:tokens - rows, :], r_send)
     for count in sorted({heads // contexts, most}):
         @pl.when(own_count == count)
         def _():
@@ -353,7 +357,8 @@
     peers = contexts * groups
     tokens = peers * rows
     most = -(-heads // contexts)
-    rates = jnp.pad(token_rates, ((0, 0), (0, 0), (0, 0), (0, 128 - token_rates.shape[3])))
+    rates = token_rates[0].transpose(1, 0, 2).reshape(rows, -1)
+    rates = jnp.pad(rates, ((0, 0), (0, -rates.shape[1] % 128)))
     gain = out_gain.astype(F32).reshape(heads, 1, dh)
     dims = (contexts, groups, heads, blocks, rows, dh, hf)
     anywhere = pl.BlockSpec(memory_space=pl.ANY)
@@ -371,7 +376,7 @@
         out_specs=(anywhere, anywhere),
         scratch_shapes=[
             later_tok, tok, tok,
-            pltpu.VMEM((blocks, tokens, 128), BF16),
+            pltpu.VMEM((tokens, rates.shape[1]), BF16),
             pltpu.VMEM((3, heads, dh, hf), BF16),
             first_tok, first_tok,
             later_tok,

time: 110 us -> 99 us (0.900)
  the two profiles are of different devices: /device:TPU:6 before, /device:TPU:0 now
where the time goes in v3:
time: 99 us; the launch traced here: 98.6 us
  Pallas kernels  88.8 us (90%)
  local copies, waits for them, and re-layouts  6.82 us (7%)
  other arithmetic  2.4 us (2%)
    pallas_call x1, Pallas kernels, body(): pl.pallas_call(functools.partial(kernel, dims), out_shape=(jax.ShapeDtype...  88.8 us
    unnamed x9, local copies, waits for them, and re-layouts  5.29 us
    broadcast_in_dim x1, other arithmetic, body(): return (head_out, final.astype(F32)[None])  2.4 us

profile of v3, /device:TPU:0, one launch (start us, length us, event | category | flops | bytes accessed | tf_op | source)
XLA Modules:
  0.0 98.6 jit_solution(3241345603453155711)
XLA Ops:
  0.6 0.7 reshape.16.gain_ref
  1.3 0.7 copy.8
  2.1 0.1 reshape.12
  2.2 0.0 copy-start
  2.2 1.2 %copy-done = bf16[3,10,64,256]{3,2,1,0:T(8,128)(2,1)S(1)} copy-done((bf16[3,10,64,256]{3,2,1,0:T(8,128)(2,1)S(1)}, bf16[3,10,64,256]{3,2,1,0:T(8,128)(2,1)}, u32[]{:S(2)}) %copy-start) | copy-done | bytes 983064
  3.4 0.0 copy-start.1
  3.4 1.1 %copy-done.1 = bf16[1,2,32,5120]{3,2,1,0:T(8,128)(2,1)S(1)} copy-done((bf16[1,2,32,5120]{3,2,1,0:T(8,128)(2,1)S(1)}, bf16[1,2,32,5120]{3,2,1,0:T(8,128)(2,1)}, u32[]{:S(2)}) %copy-start.1) | copy-done | bytes 655384
  4.5 0.0 copy-start.2
  4.5 1.1 %copy-done.2 = bf16[1,2,32,5120]{3,2,1,0:T(8,128)(2,1)S(1)} copy-done((bf16[1,2,32,5120]{3,2,1,0:T(8,128)(2,1)S(1)}, bf16[1,2,32,5120]{3,2,1,0:T(8,128)(2,1)}, u32[]{:S(2)}) %copy-start.2) | copy-done | bytes 655384
  5.5 0.0 copy-start.3
  5.5 1.1 %copy-done.3 = bf16[1,2,32,5120]{3,2,1,0:T(8,128)(2,1)S(1)} copy-done((bf16[1,2,32,5120]{3,2,1,0:T(8,128)(2,1)S(1)}, bf16[1,2,32,5120]{3,2,1,0:T(8,128)(2,1)}, u32[]{:S(2)}) %copy-start.3) | copy-done | bytes 655384
  6.6 88.8 %shard_map.77 = (bf16[1,2,128,1280]{3,2,1,0:T(8,128)(2,1)S(1)}, bf16[3,10,128,256]{3,2,1,0:T(8,128)(2,1)S(1)}) custom-call(bf16[1,2,32,5120]{3,2,1,0:T(8,128)(2,1)S(1)} %copy-done.1, bf16[1,2,32,5120]{3,2,1,0:T(8,128)(2,1)S(1)} %copy-done.2, bf16[1,2,32,5120]{3,2,1,0:T(8,128)(2,1)S(1)} %copy-done.3, bf16[32,128]{1,0:T(8,128)(2,1)S(1)} %pad.4.r_ref, ...), custom_call_target="tpu_custom_call" | custom-call | tf_op jit(solution)/shard_map/pallas_call | solution.py:369
  95.4 2.4 %bitcast_convert_fusion = f32[1,3,10,128,256]{4,3,2,1,0:T(8,128)} fusion(bf16[3,10,128,256]{3,2,1,0:T(8,128)(2,1)S(1)} %get-tuple-element.5), kind=kLoop, calls=%fused_computation | loop fusion | flops 983040 | bytes 5898240 | tf_op jit(solution)/shard_map/broadcast_in_dim | solution.py:394
  97.8 0.8 copy.10
  (1 shorter events, 0.0 us)
Async XLA Ops:
  2.2 1.2 %copy-start = (bf16[3,10,64,256]{3,2,1,0:T(8,128)(2,1)S(1)}, bf16[3,10,64,256]{3,2,1,0:T(8,128)(2,1)}, u32[]{:S(2)}) copy-start(bf16[3,10,64,256]{3,2,1,0:T(8,128)(2,1)} %w_ref.1) | copy-start | bytes 2949124
  3.4 1.1 %copy-start.1 = (bf16[1,2,32,5120]{3,2,1,0:T(8,128)(2,1)S(1)}, bf16[1,2,32,5120]{3,2,1,0:T(8,128)(2,1)}, u32[]{:S(2)}) copy-start(bf16[1,2,32,5120]{3,2,1,0:T(8,128)(2,1)} %q_ref.1) | copy-start | bytes 1966084
  4.5 1.1 %copy-start.2 = (bf16[1,2,32,5120]{3,2,1,0:T(8,128)(2,1)S(1)}, bf16[1,2,32,5120]{3,2,1,0:T(8,128)(2,1)}, u32[]{:S(2)}) copy-start(bf16[1,2,32,5120]{3,2,1,0:T(8,128)(2,1)} %k_ref.1) | copy-start | bytes 1966084
  5.5 1.1 %copy-start.3 = (bf16[1,2,32,5120]{3,2,1,0:T(8,128)(2,1)S(1)}, bf16[1,2,32,5120]{3,2,1,0:T(8,128)(2,1)}, u32[]{:S(2)}) copy-start(bf16[1,2,32,5120]{3,2,1,0:T(8,128)(2,1)} %v_ref.1) | copy-start | bytes 1966084

commit v4 on v3

--- a/solution.py
+++ b/solution.py
@@ -246,7 +246,7 @@
                 grad = g_acc[m]
                 frob = jnp.sqrt(jnp.sum(jnp.sum(grad * grad, axis=0, keepdims=True), axis=1, keepdims=True)) + 1e-07
                 ortho.append(grad / frob)
-            ortho = lax.fori_loop(0, NS_STEPS, lambda s, xs: tuple(schulz_step(x) for x in xs), tuple(ortho))
+            ortho = lax.fori_loop(0, NS_STEPS, lambda s, xs: tuple(schulz_step(x) for x in xs), tuple(ortho), unroll=True)
             for m in range(3):
                 moved = w_now[m] + eta * ortho[m]
                 scale = norms[m] * lax.rsqrt(jnp.sum(moved * moved, axis=0, keepdims=True) + 1e-06)

time: 99 us -> 97.4 us (0.984)
  Pallas kernels: 88.8 us -> 87.2 us
    pallas_call x1, Pallas kernels: 88.8 us -> 87.2 us  [body(): pl.pallas_call(functools.partial(kernel, dims), out_shape=(jax.ShapeDtype...]
where the time goes in v4:
time: 97.4 us; the launch traced here: 97 us
  Pallas kernels  87.2 us (90%)
  local copies, waits for them, and re-layouts  6.82 us (7%)
  other arithmetic  2.4 us (2%)
    pallas_call x1, Pallas kernels, body(): pl.pallas_call(functools.partial(kernel, dims), out_shape=(jax.ShapeDtype...  87.2 us
    unnamed x9, local copies, waits for them, and re-layouts  5.29 us
    broadcast_in_dim x1, other arithmetic, body(): return (head_out, final.astype(F32)[None])  2.4 us

profile of v4, /device:TPU:0, one launch (start us, length us, event | category | flops | bytes accessed | tf_op | source)
XLA Modules:
  0.0 97.0 jit_solution(15664923967068258920)
XLA Ops:
  0.6 0.7 reshape.16.gain_ref
  1.3 0.7 copy.8
  2.1 0.1 reshape.12
  2.2 0.0 copy-start
  2.2 1.2 %copy-done = bf16[3,10,64,256]{3,2,1,0:T(8,128)(2,1)S(1)} copy-done((bf16[3,10,64,256]{3,2,1,0:T(8,128)(2,1)S(1)}, bf16[3,10,64,256]{3,2,1,0:T(8,128)(2,1)}, u32[]{:S(2)}) %copy-start) | copy-done | bytes 983064
  3.4 0.0 copy-start.1
  3.4 1.1 %copy-done.1 = bf16[1,2,32,5120]{3,2,1,0:T(8,128)(2,1)S(1)} copy-done((bf16[1,2,32,5120]{3,2,1,0:T(8,128)(2,1)S(1)}, bf16[1,2,32,5120]{3,2,1,0:T(8,128)(2,1)}, u32[]{:S(2)}) %copy-start.1) | copy-done | bytes 655384
  4.5 0.0 copy-start.2
  4.5 1.1 %copy-done.2 = bf16[1,2,32,5120]{3,2,1,0:T(8,128)(2,1)S(1)} copy-done((bf16[1,2,32,5120]{3,2,1,0:T(8,128)(2,1)S(1)}, bf16[1,2,32,5120]{3,2,1,0:T(8,128)(2,1)}, u32[]{:S(2)}) %copy-start.2) | copy-done | bytes 655384
  5.5 0.0 copy-start.3
  5.5 1.1 %copy-done.3 = bf16[1,2,32,5120]{3,2,1,0:T(8,128)(2,1)S(1)} copy-done((bf16[1,2,32,5120]{3,2,1,0:T(8,128)(2,1)S(1)}, bf16[1,2,32,5120]{3,2,1,0:T(8,128)(2,1)}, u32[]{:S(2)}) %copy-start.3) | copy-done | bytes 655384
  6.6 87.2 %shard_map.77 = (bf16[1,2,128,1280]{3,2,1,0:T(8,128)(2,1)S(1)}, bf16[3,10,128,256]{3,2,1,0:T(8,128)(2,1)S(1)}) custom-call(bf16[1,2,32,5120]{3,2,1,0:T(8,128)(2,1)S(1)} %copy-done.1, bf16[1,2,32,5120]{3,2,1,0:T(8,128)(2,1)S(1)} %copy-done.2, bf16[1,2,32,5120]{3,2,1,0:T(8,128)(2,1)S(1)} %copy-done.3, bf16[32,128]{1,0:T(8,128)(2,1)S(1)} %pad.4.r_ref, ...), custom_call_target="tpu_custom_call" | custom-call | tf_op jit(solution)/shard_map/pallas_call | solution.py:369
  93.8 2.4 %bitcast_convert_fusion = f32[1,3,10,128,256]{4,3,2,1,0:T(8,128)} fusion(bf16[3,10,128,256]{3,2,1,0:T(8,128)(2,1)S(1)} %get-tuple-element.5), kind=kLoop, calls=%fused_computation | loop fusion | flops 983040 | bytes 5898240 | tf_op jit(solution)/shard_map/broadcast_in_dim | solution.py:394
  96.2 0.8 copy.10
  (1 shorter events, 0.0 us)
Async XLA Ops:
  2.2 1.2 %copy-start = (bf16[3,10,64,256]{3,2,1,0:T(8,128)(2,1)S(1)}, bf16[3,10,64,256]{3,2,1,0:T(8,128)(2,1)}, u32[]{:S(2)}) copy-start(bf16[3,10,64,256]{3,2,1,0:T(8,128)(2,1)} %w_ref.1) | copy-start | bytes 2949124
  3.4 1.1 %copy-start.1 = (bf16[1,2,32,5120]{3,2,1,0:T(8,128)(2,1)S(1)}, bf16[1,2,32,5120]{3,2,1,0:T(8,128)(2,1)}, u32[]{:S(2)}) copy-start(bf16[1,2,32,5120]{3,2,1,0:T(8,128)(2,1)} %q_ref.1) | copy-start | bytes 1966084
  4.5 1.1 %copy-start.2 = (bf16[1,2,32,5120]{3,2,1,0:T(8,128)(2,1)S(1)}, bf16[1,2,32,5120]{3,2,1,0:T(8,128)(2,1)}, u32[]{:S(2)}) copy-start(bf16[1,2,32,5120]{3,2,1,0:T(8,128)(2,1)} %k_ref.1) | copy-start | bytes 1966084
  5.5 1.1 %copy-start.3 = (bf16[1,2,32,5120]{3,2,1,0:T(8,128)(2,1)S(1)}, bf16[1,2,32,5120]{3,2,1,0:T(8,128)(2,1)}, u32[]{:S(2)}) copy-start(bf16[1,2,32,5120]{3,2,1,0:T(8,128)(2,1)} %v_ref.1) | copy-start | bytes 1966084
